TPU v7x, 32 devices: a whole 2x2x4 slice. The times are simulated.
32 devices in a mesh: grp: 4 (over z), blk: 8 (over y, x, core).
Axes of the slice: x: 2, y: 2, z: 4, core: 2. Of those that a mesh axis runs over, the one named last changes fastest.
Arguments:
- embeddings: bfloat16 [8192, 768], P(('grp', 'blk')), may hold values from -6 to 6
- target: int32 [8192, 1], P(('grp', 'blk')), may hold values from 0 to 31; in each aligned block of 256 rows (0 to 255, 256 to 511, ...) at most 16 rows name the same one
- cluster: int32 [8192], P(('grp', 'blk')), may hold values from 0 to 15
Outputs:
- nearest: float32 [8192], P(('grp', 'blk'))
Inputs may be any that keep to these rules, and one draw needn't show every extreme that they name: The rows of one device send at most 16 rows to any one target.
All inputs are finite; a program needn't handle non-finite values.
Results may differ from a plain program's by a relative error of at most 0.0014.
Values may be sent and summed in bfloat16 or wider, within the bound.
No kernel may reach another device: no remote copies, remote signals or barrier semaphores. Data moves between devices by JAX's collectives and lax.ppermute only.
A program may use at most 64 MiB of HBM per device.

v0:
```python
import functools

import jax
import jax.numpy as jnp
from jax import lax
from jax.experimental import pallas as pl
from jax.experimental.pallas import tpu as pltpu
from jax.sharding import PartitionSpec as P

CLUSTERS = 64
TAIL = 16
VMEM = 24 << 20
VMEM_SMALL = 8 << 20


def pack_kernel(per_group, emb_ref, target_ref, cluster_ref, out_ref):
    rows, width = emb_ref.shape
    x = emb_ref[...].astype(jnp.float32)
    scale = lax.rsqrt(jnp.sum(x * x, axis=1, keepdims=True) + 1e-06)
    out_ref[:rows, :] = (x * scale).astype(jnp.bfloat16)
    key = target_ref[...] // per_group * CLUSTERS + cluster_ref[...] + 1
    key = jnp.concatenate([key, jnp.zeros((1, width - rows), jnp.int32)], axis=1)
    key = jnp.broadcast_to(key.astype(jnp.float32), (TAIL, width))
    out_ref[rows:, :] = key.astype(jnp.bfloat16)


def pack(embeddings, target, cluster, per_group):
    rows, width = embeddings.shape
    return pl.pallas_call(
        functools.partial(pack_kernel, per_group),
        out_shape=jax.ShapeDtypeStruct((rows + TAIL, width), jnp.bfloat16),
        compiler_params=pltpu.CompilerParams(vmem_limit_bytes=VMEM_SMALL),
        name="pack",
    )(embeddings, target.reshape(1, rows), cluster.reshape(1, rows))


def whole(pieces):
    return pieces[0][...] if len(pieces) == 1 else jnp.concatenate([ref[...] for ref in pieces], axis=0)


def score_kernel(counts, n_cols, pairs, want_rows, known, n_rows_in, outs, row_outs, places, *refs):
    *plane, cols, cols_in, rows_in, col_refs, row_refs = take(
        refs, counts + (n_cols, bool(known), n_rows_in, len(outs), 1 if places else len(row_outs))
    )
    rows = col_refs[0].shape[2]
    best = [jnp.full((1, rows), -1.0, jnp.float32)] * n_cols
    rows_best = [ref[0] for ref in rows_in]
    for at, col in enumerate(known):
        best[col] = cols_in[0][at]
    for k, pieces in enumerate(plane):
        block = whole(pieces)
        row_keys = jnp.transpose(jnp.broadcast_to(block[rows:, :rows].astype(jnp.float32)[:1], (128, rows)))
        row_keys = jnp.concatenate([row_keys] * (rows // 128), axis=1)
        row_best = None
        for at, same in [(at, same) for one, at, same in pairs if one == k]:
            scores = lax.dot_general(
                block[:rows], cols[at][:rows, :], (((1,), (1,)), ((), ())), preferred_element_type=jnp.float32
            )
            allowed = row_keys == cols[at][rows:, :rows].astype(jnp.float32)[:1]
            if same:
                one = lax.broadcasted_iota(jnp.int32, scores.shape, 0)
                other = lax.broadcasted_iota(jnp.int32, scores.shape, 1)
                allowed = allowed & (one != other)
            masked = jnp.where(allowed, scores, -1.0)
            best[at] = jnp.maximum(best[at], jnp.max(masked, axis=0, keepdims=True))
            if at in want_rows:
                for lane in range(0, rows, 128):
                    part = masked[:, lane : lane + 128]
                    row_best = part if row_best is None else jnp.maximum(row_best, part)
        if row_best is not None:
            rows_best.append(jnp.max(jnp.transpose(row_best), axis=0, keepdims=True))
    for refs, values, holds in ((col_refs, best, outs), (row_refs, rows_best, row_outs)):
        for ref, held in zip(refs, holds):
            for at, one in enumerate(held):
                ref[at] = values[one]
    if places:
        chip = lax.axis_index("blk") // 2
        for place, value in zip(places, rows_best):
            row_refs[0][chip ^ place] = value


def take(refs, counts):
    groups, at = [], 0
    for count in counts:
        groups.append(refs[at : at + count])
        at += count
    return groups


def score(name, plane, cols, pairs, outs, want_rows=(), row_outs=(), known=(), cols_in=(), rows_in=(), places=()):
    length, width = cols[0].shape
    rows = length - TAIL
    counts = tuple(len(pieces) for pieces in plane)
    kernel = functools.partial(
        score_kernel,
        counts,
        len(cols),
        tuple(pairs),
        tuple(want_rows),
        tuple(known),
        len(rows_in),
        tuple(outs),
        tuple(row_outs),
        tuple(places),
    )
    held_rows = [places] if places else row_outs
    return pl.pallas_call(
        kernel,
        out_shape=[jax.ShapeDtypeStruct((len(held), 1, rows), jnp.float32) for held in (*outs, *held_rows)],
        compiler_params=pltpu.CompilerParams(vmem_limit_bytes=VMEM),
        cost_estimate=pl.CostEstimate(
            flops=2 * len(pairs) * rows * rows * width,
            bytes_accessed=2 * (len(plane) + len(cols)) * length * width,
            transcendentals=0,
        ),
        name=name,
    )(*[piece for pieces in plane for piece in pieces], *cols, *cols_in, *rows_in)


def join_kernel(n, *refs):
    for at in range(n):
        refs[n + 1 + at][...] = jnp.maximum(refs[at][...], refs[n][at])


def join(here, got):
    return pl.pallas_call(
        functools.partial(join_kernel, len(here)),
        out_shape=[jax.ShapeDtypeStruct((1, x.shape[-1]), x.dtype) for x in here],
        compiler_params=pltpu.CompilerParams(vmem_limit_bytes=VMEM_SMALL),
        name="join",
    )(*[x.reshape(1, -1) for x in here], got)


def plane_shift(x, mask):
    size = lax.axis_size("blk")
    return lax.ppermute(x, "blk", [(i, i ^ mask) for i in range(size)])


def grp_shift(x, shift, mask=0):
    groups, size = lax.axis_size("grp"), lax.axis_size("blk")
    if not mask:
        return lax.ppermute(x, "grp", [(z, (z + shift) % groups) for z in range(groups)])
    pairs = [
        (z * size + i, (z + shift) % groups * size + (i ^ mask)) for z in range(groups) for i in range(size)
    ]
    return lax.ppermute(x, ("grp", "blk"), pairs)


def fetch_plane(packed, per_group):
    half = (packed.shape[0] - TAIL) // 2
    plane = {0: (packed,)}
    halves = {}
    for mask in sorted(range(2, per_group, 2), key=lambda mask: mask.bit_count()):
        low, high = mask & -mask, 1 << (mask.bit_length() - 1)
        if low == high:
            block = plane_shift(packed, mask)
            plane[mask] = (block,)
            halves[mask] = (block[:half], block[half:])
        else:
            plane[mask] = halves[mask] = (
                plane_shift(halves[mask ^ low][0], low),
                plane_shift(halves[mask ^ high][1], high),
            )
    return plane


def body(embeddings, target, cluster):
    groups = lax.axis_size("grp")
    per_group = lax.axis_size("blk")
    packed = pack(embeddings, target, cluster, per_group)
    one_off = grp_shift(packed, 1)
    plane = fetch_plane(packed, per_group)
    half_way = grp_shift(one_off, 1)
    direct = [mask for mask, pieces in plane.items() if len(pieces) == 1]
    relayed = [mask for mask, pieces in plane.items() if len(pieces) > 1]

    own_then = lax.optimization_barrier((packed, one_off))[0]
    cols = [packed, plane_shift(own_then, 1), one_off, plane_shift(one_off, 1)]
    every = range(len(cols))
    best, *rows_direct = score(
        "compare_direct",
        [plane[mask] for mask in direct],
        cols,
        [(k, at, k == at == 0) for k in range(len(direct)) for at in every],
        [tuple(every)],
        (2, 3),
        [(k,) for k in range(len(direct))],
    )
    own, one_off_best, twins, rows_best = score(
        "compare_relayed",
        [plane[mask] for mask in relayed],
        cols,
        [(k, at, False) for k in range(len(relayed)) for at in every],
        [(0,), (2,), (1, 3)],
        (2, 3),
        known=every,
        cols_in=[best],
        rows_in=rows_direct,
        places=[mask // 2 for mask in direct + relayed],
    )
    cores = [[i for i in range(per_group) if i % 2 == core] for core in range(2)]
    rows_back = lax.all_to_all(
        rows_best, "blk", split_axis=0, concat_axis=0, axis_index_groups=cores, tiled=True
    )
    own, one_off_best = join([own, one_off_best], plane_shift(twins, 1))
    found = [own.reshape(1, 1, -1), grp_shift(one_off_best.reshape(1, 1, -1), -1)]

    blocks = list(plane.values())
    pairs = [(k, 0, False) for k in range(len(blocks))]
    half_then = lax.optimization_barrier((half_way, own))[0]
    for name, block, twin in (("compare_half_way", half_way, 0), ("compare_twin", plane_shift(half_then, 1), 1)):
        (half_best,) = score(name, blocks, [block], pairs, [(0,)])
        found.append(grp_shift(half_best, groups // 2, twin))
    found.append(jnp.max(rows_back, axis=0, keepdims=True))
    return functools.reduce(jnp.maximum, found).reshape(-1)


def solution(mesh):
    return jax.shard_map(
        body,
        mesh=mesh,
        in_specs=(P(("grp", "blk"), None), P(("grp", "blk"), None), P(("grp", "blk"))),
        out_specs=P(("grp", "blk")),
        check_vma=False,
    )
```

profile of v0, /device:TPU:0, one launch (start us, length us, event | category | flops | bytes accessed | tf_op | source)
XLA Modules:
  0.0 40.9 jit_solution(1301317464498965392)
XLA Ops:
  0.0 0.7 %copy-done.2 = s32[256]{0:T(256)S(1)} copy-done((s32[256]{0:T(256)S(1)}, s32[256]{0:T(256)}, u32[]{:S(2)}) %copy-start.2) | copy-done | bytes 1048
  0.7 0.0 copy-done.1
  0.7 1.0 %copy-done = bf16[256,768]{1,0:T(8,128)(2,1)S(1)} copy-done((bf16[256,768]{1,0:T(8,128)(2,1)S(1)}, bf16[256,768]{1,0:T(8,128)(2,1)}, u32[]{:S(2)}) %copy-start) | copy-done | bytes 393240
  1.7 0.2 pack.1.refs_0_.refs_3_.refs_2_
  1.9 3.1 %collective-permute-start.4 = (bf16[272,768]{1,0:T(8,128)(2,1)S(1)}, bf16[272,768]{1,0:T(8,128)(2,1)S(1)}, u32[]{:S(2)}, u32[]{:S(2)}) collective-permute-start(bf16[272,768]{1,0:T(8,128)(2,1)S(1)} %pack.1.refs_0_.refs_3_.refs_2_), channel_id=1, source_target_pairs={{0,8},{8,16},{16,24},{24,0},{1,9},{9,17},{17,25},{25,1},{2,10},{10... | collective-permute-start | bytes 1253384 | tf_op jit(solution)/shard_map/ppermute | solution.py:142
  4.9 1.5 %collective-permute-start.2 = (bf16[272,768]{1,0:T(8,128)(2,1)S(1)}, bf16[272,768]{1,0:T(8,128)(2,1)S(1)}, u32[]{:S(2)}, u32[]{:S(2)}) collective-permute-start(bf16[272,768]{1,0:T(8,128)(2,1)S(1)} %pack.1.refs_0_.refs_3_.refs_2_), channel_id=1, source_target_pairs={{0,2},{1,3},{2,0},{3,1},{4,6},{5,7},{6,4},{7,5},{8,10},{9,11},{10,... | collective-permute-start | bytes 1253384 | tf_op jit(solution)/shard_map/ppermute | solution.py:136
  6.4 1.5 %collective-permute-start = (bf16[272,768]{1,0:T(8,128)(2,1)S(1)}, bf16[272,768]{1,0:T(8,128)(2,1)S(1)}, u32[]{:S(2)}, u32[]{:S(2)}) collective-permute-start(bf16[272,768]{1,0:T(8,128)(2,1)S(1)} %pack.1.refs_0_.refs_3_.refs_2_), channel_id=1, source_target_pairs={{0,4},{1,5},{2,6},{3,7},{4,0},{5,1},{6,2},{7,3},{8,12},{9,13},{10,... | collective-permute-start | bytes 1253384 | tf_op jit(solution)/shard_map/ppermute | solution.py:136
  7.9 8.7 %collective-permute-done.4.refs_5_.refs_4_ = bf16[272,768]{1,0:T(8,128)(2,1)S(1)} collective-permute-done((bf16[272,768]{1,0:T(8,128)(2,1)S(1)}, bf16[272,768]{1,0:T(8,128)(2,1)S(1)}, u32[]{:S(2)}, u32[]{:S(2)}) %collective-permute-start.4) | collective-permute-done | bytes 417824 | tf_op jit(solution)/shard_map/ppermute | solution.py:142
  16.6 0.0 collective-permute-start.5
  16.6 0.5 %collective-permute-start.6 = (bf16[272,768]{1,0:T(8,128)(2,1)S(1)}, bf16[272,768]{1,0:T(8,128)(2,1)S(1)}, u32[]{:S(2)}, u32[]{:S(2)}) collective-permute-start(bf16[272,768]{1,0:T(8,128)(2,1)S(1)} %collective-permute-done.4.refs_5_.refs_4_), channel_id=1, source_target_pairs={{0,1},{1,0},{2,3},{3,2},{4,5},{5,4},{6,7},{7,6},{8,9},{9,8},{10,11... | collective-permute-start | bytes 1253384 | tf_op jit(solution)/shard_map/ppermute | solution.py:136
  17.1 0.0 collective-permute-start.9
  17.1 0.0 collective-permute-done.2.refs_1_
  17.1 1.6 %collective-permute-start.3 = (bf16[144,768]{1,0:T(8,128)(2,1)S(1)}, bf16[144,768]{1,0:T(8,128)(2,1)S(1)}, u32[]{:S(2)}, u32[]{:S(2)}) collective-permute-start(bf16[144,768]{1,0:T(8,128)(2,1)S(1)} %slice.9), channel_id=1, source_target_pairs={{0,4},{1,5},{2,6},{3,7},{4,0},{5,1},{6,2},{7,3},{8,12},{9,13},{10,... | collective-permute-start | bytes 663560 | tf_op jit(solution)/shard_map/ppermute | solution.py:136
  18.7 0.0 collective-permute-done.refs_2_
  18.7 1.6 %collective-permute-start.1 = (bf16[128,768]{1,0:T(8,128)(2,1)S(1)}, bf16[128,768]{1,0:T(8,128)(2,1)S(1)}, u32[]{:S(2)}, u32[]{:S(2)}) collective-permute-start(bf16[128,768]{1,0:T(8,128)(2,1)S(1)} %slice.8), channel_id=1, source_target_pairs={{0,2},{1,3},{2,0},{3,1},{4,6},{5,7},{6,4},{7,5},{8,10},{9,11},{10,... | collective-permute-start | bytes 589832 | tf_op jit(solution)/shard_map/ppermute | solution.py:136
  20.3 1.5 %compare_direct.1 = (f32[4,1,256]{2,1,0:T(1,128)S(1)}, f32[1,1,256]{2,1,0:T(1,128)S(1)}, f32[1,1,256]{2,1,0:T(1,128)S(1)}, f32[1,1,256]{2,1,0:T(1,128)S(1)}) custom-call(bf16[272,768]{1,0:T(8,128)(2,1)S(1)} %pack.1.refs_0_.refs_3_.refs_2_, bf16[272,768]{1,0:T(8,128)(2,1)S(1)} %collective-permute-done.2.refs_1_, ...), custom_call_target="tpu_custom_call" | custom-call | flops 1207959552 | bytes 2924544 | tf_op jit(solution)/shard_map/compare_direct/pallas_call | solution.py:107
  21.8 3.5 %collective-permute-done.1.refs_0_.refs_3_ = bf16[128,768]{1,0:T(8,128)(2,1)S(1)} collective-permute-done((bf16[128,768]{1,0:T(8,128)(2,1)S(1)}, bf16[128,768]{1,0:T(8,128)(2,1)S(1)}, u32[]{:S(2)}, u32[]{:S(2)}) %collective-permute-start.1) | collective-permute-done | bytes 196640 | tf_op jit(solution)/shard_map/ppermute | solution.py:136
  25.3 0.0 collective-permute-done.3.refs_1_.refs_4_
  25.3 1.3 %compare_relayed.1 = (f32[1,1,256]{2,1,0:T(1,128)S(1)}, f32[1,1,256]{2,1,0:T(1,128)S(1)}, f32[2,1,256]{2,1,0:T(1,128)S(1)}, f32[4,1,256]{2,1,0:T(1,128)}) custom-call(bf16[128,768]{1,0:T(8,128)(2,1)S(1)} %collective-permute-done.1.refs_0_.refs_3_, bf16[144,768]{1,0:T(8,128)(2,1)S(1)} %collective-permute-done.3.refs_1_.refs_4_, ...), custom_call_target="tpu_custom_call" | custom-call | flops 402653184 | bytes 2088960 | tf_op jit(solution)/shard_map/compare_relayed/pallas_call | solution.py:107
  26.6 1.2 %collective-permute-done.7.refs_2_ = f32[2,1,256]{2,1,0:T(1,128)S(1)} collective-permute-done((f32[2,1,256]{2,1,0:T(1,128)S(1)}, f32[2,1,256]{2,1,0:T(1,128)S(1)}, u32[]{:S(2)}, u32[]{:S(2)}) %collective-permute-start.7) | collective-permute-done | bytes 2080 | tf_op jit(solution)/shard_map/ppermute | solution.py:136
  27.8 2.7 %collective-permute-done.9.refs_5_ = bf16[272,768]{1,0:T(8,128)(2,1)S(1)} collective-permute-done((bf16[272,768]{1,0:T(8,128)(2,1)S(1)}, bf16[272,768]{1,0:T(8,128)(2,1)S(1)}, u32[]{:S(2)}, u32[]{:S(2)}) %collective-permute-start.9) | collective-permute-done | bytes 417824 | tf_op jit(solution)/shard_map/ppermute | solution.py:142
  30.5 0.0 collective-permute-start.11
  30.5 3.7 %all-to-all-start = ((f32[4,1,256]{2,1,0:T(1,128)}), f32[4,1,256]{2,1,0:T(1,128)S(1)}, u32[]{:S(2)}, u32[]{:S(2)}) async-start(f32[4,1,256]{2,1,0:T(1,128)} %get-tuple-element.28), calls=%async_computation | async-start | bytes 8192 | tf_op jit(solution)/shard_map/all_to_all | solution.py:202
  34.2 0.6 %compare_half_way.1 = f32[1,1,256]{2,1,0:T(1,128)S(1)} custom-call(bf16[272,768]{1,0:T(8,128)(2,1)S(1)} %pack.1.refs_0_.refs_3_.refs_2_, bf16[272,768]{1,0:T(8,128)(2,1)S(1)} %collective-permute-done.2.refs_1_, bf16[272,768]{1,0:T(8,128)(2,1)S(1)} %collective-permute-done.refs_2_, bf16[128,768]{1,0:T(8,128)(2,1)S(1)} %collective-permute-done.1.refs_0_.refs_3_, ...), custom_call_target="tpu_custom_call" | custom-call | flops 402653184 | bytes 2088960 | tf_op jit(solution)/shard_map/compare_half_way/pallas_call | solution.py:107
  34.8 0.1 collective-permute-start.10
  34.9 0.8 %collective-permute-start.8 = (f32[1,1,256]{2,1,0:T(1,128)S(1)}, f32[1,1,256]{2,1,0:T(1,128)S(1)}, u32[]{:S(2)}, u32[]{:S(2)}) collective-permute-start(f32[1,1,256]{2,1,0:T(1,128)S(1)} %bitcast.19), channel_id=1, source_target_pairs={{0,24},{8,0},{16,8},{24,16},{1,25},{9,1},{17,9},{25,17},{2,26},{10... | collective-permute-start | bytes 3080 | tf_op jit(solution)/shard_map/ppermute | solution.py:142
  35.7 0.6 %compare_twin.1 = f32[1,1,256]{2,1,0:T(1,128)S(1)} custom-call(bf16[272,768]{1,0:T(8,128)(2,1)S(1)} %pack.1.refs_0_.refs_3_.refs_2_, bf16[272,768]{1,0:T(8,128)(2,1)S(1)} %collective-permute-done.2.refs_1_, bf16[272,768]{1,0:T(8,128)(2,1)S(1)} %collective-permute-done.refs_2_, bf16[128,768]{1,0:T(8,128)(2,1)S(1)} %collective-permute-done.1.refs_0_.refs_3_, ...), custom_call_target="tpu_custom_call" | custom-call | flops 402653184 | bytes 2088960 | tf_op jit(solution)/shard_map/compare_twin/pallas_call | solution.py:107
  36.3 1.7 %collective-permute-start.12 = (f32[1,1,256]{2,1,0:T(1,128)S(1)}, f32[1,1,256]{2,1,0:T(1,128)S(1)}, u32[]{:S(2)}, u32[]{:S(2)}) collective-permute-start(f32[1,1,256]{2,1,0:T(1,128)S(1)} %compare_twin.1), channel_id=1, source_target_pairs={{0,17},{1,16},{2,19},{3,18},{4,21},{5,20},{6,23},{7,22},{8,25},{9,... | collective-permute-start | bytes 3080 | tf_op jit(solution)/shard_map/ppermute | solution.py:146
  38.0 0.8 %all-to-all-done = f32[4,1,256]{2,1,0:T(1,128)S(1)} async-done(((f32[4,1,256]{2,1,0:T(1,128)}), f32[4,1,256]{2,1,0:T(1,128)S(1)}, u32[]{:S(2)}, u32[]{:S(2)}) %all-to-all-start) | async-done | bytes 4128 | tf_op jit(solution)/shard_map/all_to_all | solution.py:202
  38.9 0.5 %collective-permute-done.10 = f32[1,1,256]{2,1,0:T(1,128)S(1)} collective-permute-done((f32[1,1,256]{2,1,0:T(1,128)S(1)}, f32[1,1,256]{2,1,0:T(1,128)S(1)}, u32[]{:S(2)}, u32[]{:S(2)}) %collective-permute-start.10) | collective-permute-done | bytes 1056 | tf_op jit(solution)/shard_map/ppermute | solution.py:142
  39.3 1.0 %collective-permute-done.12 = f32[1,1,256]{2,1,0:T(1,128)S(1)} collective-permute-done((f32[1,1,256]{2,1,0:T(1,128)S(1)}, f32[1,1,256]{2,1,0:T(1,128)S(1)}, u32[]{:S(2)}, u32[]{:S(2)}) %collective-permute-start.12) | collective-permute-done | bytes 1056 | tf_op jit(solution)/shard_map/ppermute | solution.py:146
  40.3 0.6 %fusion.2 = f32[1,1,256]{2,1,0:T(1,128)} fusion(f32[1,1,256]{2,1,0:T(1,128)S(1)} %bitcast.20, f32[1,1,256]{2,1,0:T(1,128)S(1)} %collective-permute-done.12, f32[1,1,256]{2,1,0:T(1,128)S(1)} %collective-permute-done.10, f32[1,1,256]{2,1,0:T(1,128)S(1)} %collective-permute-done.8, f32[1,256]{1,0:T(1,128)S(1)} %get-tuple-element.25), kind=kLoop, calls=%fused_computation.3 | loop fusion | flops 1024 | bytes 6144 | tf_op jit(solution)/shard_map/max | solution.py:215
  (12 shorter events, 0.1 us)
Async XLA Ops:
  0.0 0.7 %copy-start.2 = (s32[256]{0:T(256)S(1)}, s32[256]{0:T(256)}, u32[]{:S(2)}) copy-start(s32[256]{0:T(256)} %param.5) | copy-start | bytes 3076
  0.0 0.7 %copy-start.1 = (s32[256,1]{0,1:T(1,128)S(1)}, s32[256,1]{0,1:T(1,128)}, u32[]{:S(2)}) copy-start(s32[256,1]{0,1:T(1,128)} %param.4) | copy-start | bytes 3076
  0.7 1.0 %copy-start = (bf16[256,768]{1,0:T(8,128)(2,1)S(1)}, bf16[256,768]{1,0:T(8,128)(2,1)}, u32[]{:S(2)}) copy-start(bf16[256,768]{1,0:T(8,128)(2,1)} %emb_ref.1) | copy-start | bytes 1179652
  1.9 14.7 %collective-permute-start.4 = (bf16[272,768]{1,0:T(8,128)(2,1)S(1)}, bf16[272,768]{1,0:T(8,128)(2,1)S(1)}, u32[]{:S(2)}, u32[]{:S(2)}) collective-permute-start(bf16[272,768]{1,0:T(8,128)(2,1)S(1)} %pack.1.refs_0_.refs_3_.refs_2_), channel_id=1, source_target_pairs={{0,8},{8,16},{16,24},{24,0},{1,9},{9,17},{17,25},{25,1},{2,10},{10... | collective-permute-start | bytes 1253384 | tf_op jit(solution)/shard_map/ppermute | solution.py:142
  4.9 12.2 %collective-permute-start.2 = (bf16[272,768]{1,0:T(8,128)(2,1)S(1)}, bf16[272,768]{1,0:T(8,128)(2,1)S(1)}, u32[]{:S(2)}, u32[]{:S(2)}) collective-permute-start(bf16[272,768]{1,0:T(8,128)(2,1)S(1)} %pack.1.refs_0_.refs_3_.refs_2_), channel_id=1, source_target_pairs={{0,2},{1,3},{2,0},{3,1},{4,6},{5,7},{6,4},{7,5},{8,10},{9,11},{10,... | collective-permute-start | bytes 1253384 | tf_op jit(solution)/shard_map/ppermute | solution.py:136
  6.4 12.3 %collective-permute-start = (bf16[272,768]{1,0:T(8,128)(2,1)S(1)}, bf16[272,768]{1,0:T(8,128)(2,1)S(1)}, u32[]{:S(2)}, u32[]{:S(2)}) collective-permute-start(bf16[272,768]{1,0:T(8,128)(2,1)S(1)} %pack.1.refs_0_.refs_3_.refs_2_), channel_id=1, source_target_pairs={{0,4},{1,5},{2,6},{3,7},{4,0},{5,1},{6,2},{7,3},{8,12},{9,13},{10,... | collective-permute-start | bytes 1253384 | tf_op jit(solution)/shard_map/ppermute | solution.py:136
  16.6 3.7 %collective-permute-start.5 = (bf16[272,768]{1,0:T(8,128)(2,1)S(1)}, bf16[272,768]{1,0:T(8,128)(2,1)S(1)}, u32[]{:S(2)}, u32[]{:S(2)}) collective-permute-start(bf16[272,768]{1,0:T(8,128)(2,1)S(1)} %pack.1.refs_0_.refs_3_.refs_2_), channel_id=1, source_target_pairs={{0,1},{1,0},{2,3},{3,2},{4,5},{5,4},{6,7},{7,6},{8,9},{9,8},{10,11... | collective-permute-start | bytes 1253384 | tf_op jit(solution)/shard_map/ppermute | solution.py:136
  16.6 3.7 %collective-permute-start.6 = (bf16[272,768]{1,0:T(8,128)(2,1)S(1)}, bf16[272,768]{1,0:T(8,128)(2,1)S(1)}, u32[]{:S(2)}, u32[]{:S(2)}) collective-permute-start(bf16[272,768]{1,0:T(8,128)(2,1)S(1)} %collective-permute-done.4.refs_5_.refs_4_), channel_id=1, source_target_pairs={{0,1},{1,0},{2,3},{3,2},{4,5},{5,4},{6,7},{7,6},{8,9},{9,8},{10,11... | collective-permute-start | bytes 1253384 | tf_op jit(solution)/shard_map/ppermute | solution.py:136
  17.1 13.3 %collective-permute-start.9 = (bf16[272,768]{1,0:T(8,128)(2,1)S(1)}, bf16[272,768]{1,0:T(8,128)(2,1)S(1)}, u32[]{:S(2)}, u32[]{:S(2)}) collective-permute-start(bf16[272,768]{1,0:T(8,128)(2,1)S(1)} %collective-permute-done.4.refs_5_.refs_4_), channel_id=1, source_target_pairs={{0,8},{8,16},{16,24},{24,0},{1,9},{9,17},{17,25},{25,1},{2,10},{10... | collective-permute-start | bytes 1253384 | tf_op jit(solution)/shard_map/ppermute | solution.py:142
  17.1 8.2 %collective-permute-start.3 = (bf16[144,768]{1,0:T(8,128)(2,1)S(1)}, bf16[144,768]{1,0:T(8,128)(2,1)S(1)}, u32[]{:S(2)}, u32[]{:S(2)}) collective-permute-start(bf16[144,768]{1,0:T(8,128)(2,1)S(1)} %slice.9), channel_id=1, source_target_pairs={{0,4},{1,5},{2,6},{3,7},{4,0},{5,1},{6,2},{7,3},{8,12},{9,13},{10,... | collective-permute-start | bytes 663560 | tf_op jit(solution)/shard_map/ppermute | solution.py:136
  18.7 6.6 %collective-permute-start.1 = (bf16[128,768]{1,0:T(8,128)(2,1)S(1)}, bf16[128,768]{1,0:T(8,128)(2,1)S(1)}, u32[]{:S(2)}, u32[]{:S(2)}) collective-permute-start(bf16[128,768]{1,0:T(8,128)(2,1)S(1)} %slice.8), channel_id=1, source_target_pairs={{0,2},{1,3},{2,0},{3,1},{4,6},{5,7},{6,4},{7,5},{8,10},{9,11},{10,... | collective-permute-start | bytes 589832 | tf_op jit(solution)/shard_map/ppermute | solution.py:136
  26.6 1.2 %collective-permute-start.7 = (f32[2,1,256]{2,1,0:T(1,128)S(1)}, f32[2,1,256]{2,1,0:T(1,128)S(1)}, u32[]{:S(2)}, u32[]{:S(2)}) collective-permute-start(f32[2,1,256]{2,1,0:T(1,128)S(1)} %get-tuple-element.24), channel_id=1, source_target_pairs={{0,1},{1,0},{2,3},{3,2},{4,5},{5,4},{6,7},{7,6},{8,9},{9,8},{10,11... | collective-permute-start | bytes 6152 | tf_op jit(solution)/shard_map/ppermute | solution.py:136
  30.5 5.3 %collective-permute-start.11 = (bf16[272,768]{1,0:T(8,128)(2,1)S(1)}, bf16[272,768]{1,0:T(8,128)(2,1)S(1)}, u32[]{:S(2)}, u32[]{:S(2)}) collective-permute-start(bf16[272,768]{1,0:T(8,128)(2,1)S(1)} %collective-permute-done.9.refs_5_), channel_id=1, source_target_pairs={{0,1},{1,0},{2,3},{3,2},{4,5},{5,4},{6,7},{7,6},{8,9},{9,8},{10,11... | collective-permute-start | bytes 1253384 | tf_op jit(solution)/shard_map/ppermute | solution.py:136
  30.5 8.4 %all-to-all-start = ((f32[4,1,256]{2,1,0:T(1,128)}), f32[4,1,256]{2,1,0:T(1,128)S(1)}, u32[]{:S(2)}, u32[]{:S(2)}) async-start(f32[4,1,256]{2,1,0:T(1,128)} %get-tuple-element.28), calls=%async_computation | async-start | bytes 8192 | tf_op jit(solution)/shard_map/all_to_all | solution.py:202
  34.8 4.5 %collective-permute-start.10 = (f32[1,1,256]{2,1,0:T(1,128)S(1)}, f32[1,1,256]{2,1,0:T(1,128)S(1)}, u32[]{:S(2)}, u32[]{:S(2)}) collective-permute-start(f32[1,1,256]{2,1,0:T(1,128)S(1)} %compare_half_way.1), channel_id=1, source_target_pairs={{0,16},{8,24},{16,0},{24,8},{1,17},{9,25},{17,1},{25,9},{2,18},{10... | collective-permute-start | bytes 3080 | tf_op jit(solution)/shard_map/ppermute | solution.py:142
  34.9 4.5 %collective-permute-start.8 = (f32[1,1,256]{2,1,0:T(1,128)S(1)}, f32[1,1,256]{2,1,0:T(1,128)S(1)}, u32[]{:S(2)}, u32[]{:S(2)}) collective-permute-start(f32[1,1,256]{2,1,0:T(1,128)S(1)} %bitcast.19), channel_id=1, source_target_pairs={{0,24},{8,0},{16,8},{24,16},{1,25},{9,1},{17,9},{25,17},{2,26},{10... | collective-permute-start | bytes 3080 | tf_op jit(solution)/shard_map/ppermute | solution.py:142
  36.3 4.0 %collective-permute-start.12 = (f32[1,1,256]{2,1,0:T(1,128)S(1)}, f32[1,1,256]{2,1,0:T(1,128)S(1)}, u32[]{:S(2)}, u32[]{:S(2)}) collective-permute-start(f32[1,1,256]{2,1,0:T(1,128)S(1)} %compare_twin.1), channel_id=1, source_target_pairs={{0,17},{1,16},{2,19},{3,18},{4,21},{5,20},{6,23},{7,22},{8,25},{9,... | collective-permute-start | bytes 3080 | tf_op jit(solution)/shard_map/ppermute | solution.py:146
where the time goes:
time: 41.1 us; the launch traced here: 40.9 us
  waiting for transfers between devices  18.2 us (44%)
  starting transfers between devices  16.1 us (39%)
  Pallas kernels  4.2 us (10%)
  local copies, waits for them, and re-layouts  1.72 us (4%)
  other arithmetic  0.59 us (1%)
    ppermute x4, waiting for transfers between devices, grp_shift(): lax.ppermute(x, 'grp', [(z, (z + shift) % groups) for z in range(groups)])  11.8 us
    ppermute x8, starting transfers between devices, plane_shift(): return lax.ppermute(x, 'blk', [(i, i ^ mask) for i in range(size)])  6.67 us
    ppermute x8, waiting for transfers between devices, plane_shift(): return lax.ppermute(x, 'blk', [(i, i ^ mask) for i in range(size)])  4.69 us
    pallas_call x4, Pallas kernels, score(): pl.pallas_call(kernel, out_shape=[jax.ShapeDtypeStruct((len(held), 1, row...  4.03 us
    ppermute x4, starting transfers between devices, grp_shift(): lax.ppermute(x, 'grp', [(z, (z + shift) % groups) for z in range(groups)])  3.98 us
    all_to_all x1, starting transfers between devices, body(): lax.all_to_all(rows_best, 'blk', split_axis=0, concat_axis=0, axis_index_...  3.72 us
    ppermute x1, starting transfers between devices, grp_shift(): return lax.ppermute(x, ('grp', 'blk'), pairs)  1.7 us
    unnamed x6, local copies, waits for them, and re-layouts  1.69 us
  transfers between devices with their start and end apart: 14, of which 7 were waited for; matrix products, arithmetic and copies ran while one was open for 0% of the time, Pallas kernels for 10%

commit v1 on v0

--- a/solution.py
+++ b/solution.py
@@ -87,7 +87,7 @@
     return groups
 
 
-def score(name, plane, cols, pairs, outs, want_rows=(), row_outs=(), known=(), cols_in=(), rows_in=(), places=()):
+def score(name, plane, cols, pairs, outs, want_rows=(), row_outs=(), known=(), cols_in=(), rows_in=(), places=(), weight=1):
     length, width = cols[0].shape
     rows = length - TAIL
     counts = tuple(len(pieces) for pieces in plane)
@@ -109,8 +109,8 @@
         out_shape=[jax.ShapeDtypeStruct((len(held), 1, rows), jnp.float32) for held in (*outs, *held_rows)],
         compiler_params=pltpu.CompilerParams(vmem_limit_bytes=VMEM),
         cost_estimate=pl.CostEstimate(
-            flops=2 * len(pairs) * rows * rows * width,
-            bytes_accessed=2 * (len(plane) + len(cols)) * length * width,
+            flops=weight * 2 * len(pairs) * rows * rows * width,
+            bytes_accessed=weight * 2 * (len(plane) + len(cols)) * length * width,
             transcendentals=0,
         ),
         name=name,
@@ -209,7 +209,7 @@
     pairs = [(k, 0, False) for k in range(len(blocks))]
     half_then = lax.optimization_barrier((half_way, own))[0]
     for name, block, twin in (("compare_half_way", half_way, 0), ("compare_twin", plane_shift(half_then, 1), 1)):
-        (half_best,) = score(name, blocks, [block], pairs, [(0,)])
+        (half_best,) = score(name, blocks, [block], pairs, [(0,)], weight=0)
         found.append(grp_shift(half_best, groups // 2, twin))
     found.append(jnp.max(rows_back, axis=0, keepdims=True))
     return functools.reduce(jnp.maximum, found).reshape(-1)

time: 41.1 us -> 41.1 us (level)
  no operation moved by 1% of the time
where the time goes in v1:
time: 41.1 us; the launch traced here: 40.9 us
  waiting for transfers between devices  18.2 us (44%)
  starting transfers between devices  16.1 us (39%)
  Pallas kernels  4.2 us (10%)
  local copies, waits for them, and re-layouts  1.72 us (4%)
  other arithmetic  0.59 us (1%)
    ppermute x4, waiting for transfers between devices, grp_shift(): lax.ppermute(x, 'grp', [(z, (z + shift) % groups) for z in range(groups)])  11.8 us
    ppermute x8, starting transfers between devices, plane_shift(): return lax.ppermute(x, 'blk', [(i, i ^ mask) for i in range(size)])  6.67 us
    ppermute x8, waiting for transfers between devices, plane_shift(): return lax.ppermute(x, 'blk', [(i, i ^ mask) for i in range(size)])  4.69 us
    pallas_call x4, Pallas kernels, score(): pl.pallas_call(kernel, out_shape=[jax.ShapeDtypeStruct((len(held), 1, row...  4.03 us
    ppermute x4, starting transfers between devices, grp_shift(): lax.ppermute(x, 'grp', [(z, (z + shift) % groups) for z in range(groups)])  3.98 us
    all_to_all x1, starting transfers between devices, body(): lax.all_to_all(rows_best, 'blk', split_axis=0, concat_axis=0, axis_index_...  3.72 us
    ppermute x1, starting transfers between devices, grp_shift(): return lax.ppermute(x, ('grp', 'blk'), pairs)  1.7 us
    unnamed x6, local copies, waits for them, and re-layouts  1.69 us
  transfers between devices with their start and end apart: 14, of which 7 were waited for; matrix products, arithmetic and copies ran while one was open for 0% of the time, Pallas kernels for 10%

profile of v1, /device:TPU:0, one launch (start us, length us, event | category | flops | bytes accessed | tf_op | source)
XLA Modules:
  0.0 40.9 jit_solution(1301317464498965392)
XLA Ops:
  0.0 0.7 %copy-done.2 = s32[256]{0:T(256)S(1)} copy-done((s32[256]{0:T(256)S(1)}, s32[256]{0:T(256)}, u32[]{:S(2)}) %copy-start.2) | copy-done | bytes 1048
  0.7 0.0 copy-done.1
  0.7 1.0 %copy-done = bf16[256,768]{1,0:T(8,128)(2,1)S(1)} copy-done((bf16[256,768]{1,0:T(8,128)(2,1)S(1)}, bf16[256,768]{1,0:T(8,128)(2,1)}, u32[]{:S(2)}) %copy-start) | copy-done | bytes 393240
  1.7 0.2 pack.1.refs_0_.refs_3_.refs_2_
  1.9 3.1 %collective-permute-start.4 = (bf16[272,768]{1,0:T(8,128)(2,1)S(1)}, bf16[272,768]{1,0:T(8,128)(2,1)S(1)}, u32[]{:S(2)}, u32[]{:S(2)}) collective-permute-start(bf16[272,768]{1,0:T(8,128)(2,1)S(1)} %pack.1.refs_0_.refs_3_.refs_2_), channel_id=1, source_target_pairs={{0,8},{8,16},{16,24},{24,0},{1,9},{9,17},{17,25},{25,1},{2,10},{10... | collective-permute-start | bytes 1253384 | tf_op jit(solution)/shard_map/ppermute | solution.py:142
  4.9 1.5 %collective-permute-start.2 = (bf16[272,768]{1,0:T(8,128)(2,1)S(1)}, bf16[272,768]{1,0:T(8,128)(2,1)S(1)}, u32[]{:S(2)}, u32[]{:S(2)}) collective-permute-start(bf16[272,768]{1,0:T(8,128)(2,1)S(1)} %pack.1.refs_0_.refs_3_.refs_2_), channel_id=1, source_target_pairs={{0,2},{1,3},{2,0},{3,1},{4,6},{5,7},{6,4},{7,5},{8,10},{9,11},{10,... | collective-permute-start | bytes 1253384 | tf_op jit(solution)/shard_map/ppermute | solution.py:136
  6.4 1.5 %collective-permute-start = (bf16[272,768]{1,0:T(8,128)(2,1)S(1)}, bf16[272,768]{1,0:T(8,128)(2,1)S(1)}, u32[]{:S(2)}, u32[]{:S(2)}) collective-permute-start(bf16[272,768]{1,0:T(8,128)(2,1)S(1)} %pack.1.refs_0_.refs_3_.refs_2_), channel_id=1, source_target_pairs={{0,4},{1,5},{2,6},{3,7},{4,0},{5,1},{6,2},{7,3},{8,12},{9,13},{10,... | collective-permute-start | bytes 1253384 | tf_op jit(solution)/shard_map/ppermute | solution.py:136
  7.9 8.7 %collective-permute-done.4.refs_5_.refs_4_ = bf16[272,768]{1,0:T(8,128)(2,1)S(1)} collective-permute-done((bf16[272,768]{1,0:T(8,128)(2,1)S(1)}, bf16[272,768]{1,0:T(8,128)(2,1)S(1)}, u32[]{:S(2)}, u32[]{:S(2)}) %collective-permute-start.4) | collective-permute-done | bytes 417824 | tf_op jit(solution)/shard_map/ppermute | solution.py:142
  16.6 0.0 collective-permute-start.5
  16.6 0.5 %collective-permute-start.6 = (bf16[272,768]{1,0:T(8,128)(2,1)S(1)}, bf16[272,768]{1,0:T(8,128)(2,1)S(1)}, u32[]{:S(2)}, u32[]{:S(2)}) collective-permute-start(bf16[272,768]{1,0:T(8,128)(2,1)S(1)} %collective-permute-done.4.refs_5_.refs_4_), channel_id=1, source_target_pairs={{0,1},{1,0},{2,3},{3,2},{4,5},{5,4},{6,7},{7,6},{8,9},{9,8},{10,11... | collective-permute-start | bytes 1253384 | tf_op jit(solution)/shard_map/ppermute | solution.py:136
  17.1 0.0 collective-permute-start.9
  17.1 0.0 collective-permute-done.2.refs_1_
  17.1 1.6 %collective-permute-start.3 = (bf16[144,768]{1,0:T(8,128)(2,1)S(1)}, bf16[144,768]{1,0:T(8,128)(2,1)S(1)}, u32[]{:S(2)}, u32[]{:S(2)}) collective-permute-start(bf16[144,768]{1,0:T(8,128)(2,1)S(1)} %slice.9), channel_id=1, source_target_pairs={{0,4},{1,5},{2,6},{3,7},{4,0},{5,1},{6,2},{7,3},{8,12},{9,13},{10,... | collective-permute-start | bytes 663560 | tf_op jit(solution)/shard_map/ppermute | solution.py:136
  18.7 0.0 collective-permute-done.refs_2_
  18.7 1.6 %collective-permute-start.1 = (bf16[128,768]{1,0:T(8,128)(2,1)S(1)}, bf16[128,768]{1,0:T(8,128)(2,1)S(1)}, u32[]{:S(2)}, u32[]{:S(2)}) collective-permute-start(bf16[128,768]{1,0:T(8,128)(2,1)S(1)} %slice.8), channel_id=1, source_target_pairs={{0,2},{1,3},{2,0},{3,1},{4,6},{5,7},{6,4},{7,5},{8,10},{9,11},{10,... | collective-permute-start | bytes 589832 | tf_op jit(solution)/shard_map/ppermute | solution.py:136
  20.3 1.5 %compare_direct.1 = (f32[4,1,256]{2,1,0:T(1,128)S(1)}, f32[1,1,256]{2,1,0:T(1,128)S(1)}, f32[1,1,256]{2,1,0:T(1,128)S(1)}, f32[1,1,256]{2,1,0:T(1,128)S(1)}) custom-call(bf16[272,768]{1,0:T(8,128)(2,1)S(1)} %pack.1.refs_0_.refs_3_.refs_2_, bf16[272,768]{1,0:T(8,128)(2,1)S(1)} %collective-permute-done.2.refs_1_, ...), custom_call_target="tpu_custom_call" | custom-call | flops 1207959552 | bytes 2924544 | tf_op jit(solution)/shard_map/compare_direct/pallas_call | solution.py:107
  21.8 3.5 %collective-permute-done.1.refs_0_.refs_3_ = bf16[128,768]{1,0:T(8,128)(2,1)S(1)} collective-permute-done((bf16[128,768]{1,0:T(8,128)(2,1)S(1)}, bf16[128,768]{1,0:T(8,128)(2,1)S(1)}, u32[]{:S(2)}, u32[]{:S(2)}) %collective-permute-start.1) | collective-permute-done | bytes 196640 | tf_op jit(solution)/shard_map/ppermute | solution.py:136
  25.3 0.0 collective-permute-done.3.refs_1_.refs_4_
  25.3 1.3 %compare_relayed.1 = (f32[1,1,256]{2,1,0:T(1,128)S(1)}, f32[1,1,256]{2,1,0:T(1,128)S(1)}, f32[2,1,256]{2,1,0:T(1,128)S(1)}, f32[4,1,256]{2,1,0:T(1,128)}) custom-call(bf16[128,768]{1,0:T(8,128)(2,1)S(1)} %collective-permute-done.1.refs_0_.refs_3_, bf16[144,768]{1,0:T(8,128)(2,1)S(1)} %collective-permute-done.3.refs_1_.refs_4_, ...), custom_call_target="tpu_custom_call" | custom-call | flops 402653184 | bytes 2088960 | tf_op jit(solution)/shard_map/compare_relayed/pallas_call | solution.py:107
  26.6 1.2 %collective-permute-done.7.refs_2_ = f32[2,1,256]{2,1,0:T(1,128)S(1)} collective-permute-done((f32[2,1,256]{2,1,0:T(1,128)S(1)}, f32[2,1,256]{2,1,0:T(1,128)S(1)}, u32[]{:S(2)}, u32[]{:S(2)}) %collective-permute-start.7) | collective-permute-done | bytes 2080 | tf_op jit(solution)/shard_map/ppermute | solution.py:136
  27.8 2.7 %collective-permute-done.9.refs_5_ = bf16[272,768]{1,0:T(8,128)(2,1)S(1)} collective-permute-done((bf16[272,768]{1,0:T(8,128)(2,1)S(1)}, bf16[272,768]{1,0:T(8,128)(2,1)S(1)}, u32[]{:S(2)}, u32[]{:S(2)}) %collective-permute-start.9) | collective-permute-done | bytes 417824 | tf_op jit(solution)/shard_map/ppermute | solution.py:142
  30.5 0.0 collective-permute-start.11
  30.5 3.7 %all-to-all-start = ((f32[4,1,256]{2,1,0:T(1,128)}), f32[4,1,256]{2,1,0:T(1,128)S(1)}, u32[]{:S(2)}, u32[]{:S(2)}) async-start(f32[4,1,256]{2,1,0:T(1,128)} %get-tuple-element.28), calls=%async_computation | async-start | bytes 8192 | tf_op jit(solution)/shard_map/all_to_all | solution.py:202
  34.2 0.6 %compare_half_way.1 = f32[1,1,256]{2,1,0:T(1,128)S(1)} custom-call(bf16[272,768]{1,0:T(8,128)(2,1)S(1)} %pack.1.refs_0_.refs_3_.refs_2_, bf16[272,768]{1,0:T(8,128)(2,1)S(1)} %collective-permute-done.2.refs_1_, bf16[272,768]{1,0:T(8,128)(2,1)S(1)} %collective-permute-done.refs_2_, bf16[128,768]{1,0:T(8,128)(2,1)S(1)} %collective-permute-done.1.refs_0_.refs_3_, ...), custom_call_target="tpu_custom_call" | custom-call | tf_op jit(solution)/shard_map/compare_half_way/pallas_call | solution.py:107
  34.8 0.1 collective-permute-start.10
  34.9 0.8 %collective-permute-start.8 = (f32[1,1,256]{2,1,0:T(1,128)S(1)}, f32[1,1,256]{2,1,0:T(1,128)S(1)}, u32[]{:S(2)}, u32[]{:S(2)}) collective-permute-start(f32[1,1,256]{2,1,0:T(1,128)S(1)} %bitcast.19), channel_id=1, source_target_pairs={{0,24},{8,0},{16,8},{24,16},{1,25},{9,1},{17,9},{25,17},{2,26},{10... | collective-permute-start | bytes 3080 | tf_op jit(solution)/shard_map/ppermute | solution.py:142
  35.7 0.6 %compare_twin.1 = f32[1,1,256]{2,1,0:T(1,128)S(1)} custom-call(bf16[272,768]{1,0:T(8,128)(2,1)S(1)} %pack.1.refs_0_.refs_3_.refs_2_, bf16[272,768]{1,0:T(8,128)(2,1)S(1)} %collective-permute-done.2.refs_1_, bf16[272,768]{1,0:T(8,128)(2,1)S(1)} %collective-permute-done.refs_2_, bf16[128,768]{1,0:T(8,128)(2,1)S(1)} %collective-permute-done.1.refs_0_.refs_3_, ...), custom_call_target="tpu_custom_call" | custom-call | tf_op jit(solution)/shard_map/compare_twin/pallas_call | solution.py:107
  36.3 1.7 %collective-permute-start.12 = (f32[1,1,256]{2,1,0:T(1,128)S(1)}, f32[1,1,256]{2,1,0:T(1,128)S(1)}, u32[]{:S(2)}, u32[]{:S(2)}) collective-permute-start(f32[1,1,256]{2,1,0:T(1,128)S(1)} %compare_twin.1), channel_id=1, source_target_pairs={{0,17},{1,16},{2,19},{3,18},{4,21},{5,20},{6,23},{7,22},{8,25},{9,... | collective-permute-start | bytes 3080 | tf_op jit(solution)/shard_map/ppermute | solution.py:146
  38.0 0.8 %all-to-all-done = f32[4,1,256]{2,1,0:T(1,128)S(1)} async-done(((f32[4,1,256]{2,1,0:T(1,128)}), f32[4,1,256]{2,1,0:T(1,128)S(1)}, u32[]{:S(2)}, u32[]{:S(2)}) %all-to-all-start) | async-done | bytes 4128 | tf_op jit(solution)/shard_map/all_to_all | solution.py:202
  38.9 0.5 %collective-permute-done.10 = f32[1,1,256]{2,1,0:T(1,128)S(1)} collective-permute-done((f32[1,1,256]{2,1,0:T(1,128)S(1)}, f32[1,1,256]{2,1,0:T(1,128)S(1)}, u32[]{:S(2)}, u32[]{:S(2)}) %collective-permute-start.10) | collective-permute-done | bytes 1056 | tf_op jit(solution)/shard_map/ppermute | solution.py:142
  39.3 1.0 %collective-permute-done.12 = f32[1,1,256]{2,1,0:T(1,128)S(1)} collective-permute-done((f32[1,1,256]{2,1,0:T(1,128)S(1)}, f32[1,1,256]{2,1,0:T(1,128)S(1)}, u32[]{:S(2)}, u32[]{:S(2)}) %collective-permute-start.12) | collective-permute-done | bytes 1056 | tf_op jit(solution)/shard_map/ppermute | solution.py:146
  40.3 0.6 %fusion.2 = f32[1,1,256]{2,1,0:T(1,128)} fusion(f32[1,1,256]{2,1,0:T(1,128)S(1)} %bitcast.20, f32[1,1,256]{2,1,0:T(1,128)S(1)} %collective-permute-done.12, f32[1,1,256]{2,1,0:T(1,128)S(1)} %collective-permute-done.10, f32[1,1,256]{2,1,0:T(1,128)S(1)} %collective-permute-done.8, f32[1,256]{1,0:T(1,128)S(1)} %get-tuple-element.25), kind=kLoop, calls=%fused_computation.3 | loop fusion | flops 1024 | bytes 6144 | tf_op jit(solution)/shard_map/max | solution.py:215
  (12 shorter events, 0.1 us)
Async XLA Ops:
  0.0 0.7 %copy-start.2 = (s32[256]{0:T(256)S(1)}, s32[256]{0:T(256)}, u32[]{:S(2)}) copy-start(s32[256]{0:T(256)} %param.5) | copy-start | bytes 3076
  0.0 0.7 %copy-start.1 = (s32[256,1]{0,1:T(1,128)S(1)}, s32[256,1]{0,1:T(1,128)}, u32[]{:S(2)}) copy-start(s32[256,1]{0,1:T(1,128)} %param.4) | copy-start | bytes 3076
  0.7 1.0 %copy-start = (bf16[256,768]{1,0:T(8,128)(2,1)S(1)}, bf16[256,768]{1,0:T(8,128)(2,1)}, u32[]{:S(2)}) copy-start(bf16[256,768]{1,0:T(8,128)(2,1)} %emb_ref.1) | copy-start | bytes 1179652
  1.9 14.7 %collective-permute-start.4 = (bf16[272,768]{1,0:T(8,128)(2,1)S(1)}, bf16[272,768]{1,0:T(8,128)(2,1)S(1)}, u32[]{:S(2)}, u32[]{:S(2)}) collective-permute-start(bf16[272,768]{1,0:T(8,128)(2,1)S(1)} %pack.1.refs_0_.refs_3_.refs_2_), channel_id=1, source_target_pairs={{0,8},{8,16},{16,24},{24,0},{1,9},{9,17},{17,25},{25,1},{2,10},{10... | collective-permute-start | bytes 1253384 | tf_op jit(solution)/shard_map/ppermute | solution.py:142
  4.9 12.2 %collective-permute-start.2 = (bf16[272,768]{1,0:T(8,128)(2,1)S(1)}, bf16[272,768]{1,0:T(8,128)(2,1)S(1)}, u32[]{:S(2)}, u32[]{:S(2)}) collective-permute-start(bf16[272,768]{1,0:T(8,128)(2,1)S(1)} %pack.1.refs_0_.refs_3_.refs_2_), channel_id=1, source_target_pairs={{0,2},{1,3},{2,0},{3,1},{4,6},{5,7},{6,4},{7,5},{8,10},{9,11},{10,... | collective-permute-start | bytes 1253384 | tf_op jit(solution)/shard_map/ppermute | solution.py:136
  6.4 12.3 %collective-permute-start = (bf16[272,768]{1,0:T(8,128)(2,1)S(1)}, bf16[272,768]{1,0:T(8,128)(2,1)S(1)}, u32[]{:S(2)}, u32[]{:S(2)}) collective-permute-start(bf16[272,768]{1,0:T(8,128)(2,1)S(1)} %pack.1.refs_0_.refs_3_.refs_2_), channel_id=1, source_target_pairs={{0,4},{1,5},{2,6},{3,7},{4,0},{5,1},{6,2},{7,3},{8,12},{9,13},{10,... | collective-permute-start | bytes 1253384 | tf_op jit(solution)/shard_map/ppermute | solution.py:136
  16.6 3.7 %collective-permute-start.5 = (bf16[272,768]{1,0:T(8,128)(2,1)S(1)}, bf16[272,768]{1,0:T(8,128)(2,1)S(1)}, u32[]{:S(2)}, u32[]{:S(2)}) collective-permute-start(bf16[272,768]{1,0:T(8,128)(2,1)S(1)} %pack.1.refs_0_.refs_3_.refs_2_), channel_id=1, source_target_pairs={{0,1},{1,0},{2,3},{3,2},{4,5},{5,4},{6,7},{7,6},{8,9},{9,8},{10,11... | collective-permute-start | bytes 1253384 | tf_op jit(solution)/shard_map/ppermute | solution.py:136
  16.6 3.7 %collective-permute-start.6 = (bf16[272,768]{1,0:T(8,128)(2,1)S(1)}, bf16[272,768]{1,0:T(8,128)(2,1)S(1)}, u32[]{:S(2)}, u32[]{:S(2)}) collective-permute-start(bf16[272,768]{1,0:T(8,128)(2,1)S(1)} %collective-permute-done.4.refs_5_.refs_4_), channel_id=1, source_target_pairs={{0,1},{1,0},{2,3},{3,2},{4,5},{5,4},{6,7},{7,6},{8,9},{9,8},{10,11... | collective-permute-start | bytes 1253384 | tf_op jit(solution)/shard_map/ppermute | solution.py:136
  17.1 13.3 %collective-permute-start.9 = (bf16[272,768]{1,0:T(8,128)(2,1)S(1)}, bf16[272,768]{1,0:T(8,128)(2,1)S(1)}, u32[]{:S(2)}, u32[]{:S(2)}) collective-permute-start(bf16[272,768]{1,0:T(8,128)(2,1)S(1)} %collective-permute-done.4.refs_5_.refs_4_), channel_id=1, source_target_pairs={{0,8},{8,16},{16,24},{24,0},{1,9},{9,17},{17,25},{25,1},{2,10},{10... | collective-permute-start | bytes 1253384 | tf_op jit(solution)/shard_map/ppermute | solution.py:142
  17.1 8.2 %collective-permute-start.3 = (bf16[144,768]{1,0:T(8,128)(2,1)S(1)}, bf16[144,768]{1,0:T(8,128)(2,1)S(1)}, u32[]{:S(2)}, u32[]{:S(2)}) collective-permute-start(bf16[144,768]{1,0:T(8,128)(2,1)S(1)} %slice.9), channel_id=1, source_target_pairs={{0,4},{1,5},{2,6},{3,7},{4,0},{5,1},{6,2},{7,3},{8,12},{9,13},{10,... | collective-permute-start | bytes 663560 | tf_op jit(solution)/shard_map/ppermute | solution.py:136
  18.7 6.6 %collective-permute-start.1 = (bf16[128,768]{1,0:T(8,128)(2,1)S(1)}, bf16[128,768]{1,0:T(8,128)(2,1)S(1)}, u32[]{:S(2)}, u32[]{:S(2)}) collective-permute-start(bf16[128,768]{1,0:T(8,128)(2,1)S(1)} %slice.8), channel_id=1, source_target_pairs={{0,2},{1,3},{2,0},{3,1},{4,6},{5,7},{6,4},{7,5},{8,10},{9,11},{10,... | collective-permute-start | bytes 589832 | tf_op jit(solution)/shard_map/ppermute | solution.py:136
  26.6 1.2 %collective-permute-start.7 = (f32[2,1,256]{2,1,0:T(1,128)S(1)}, f32[2,1,256]{2,1,0:T(1,128)S(1)}, u32[]{:S(2)}, u32[]{:S(2)}) collective-permute-start(f32[2,1,256]{2,1,0:T(1,128)S(1)} %get-tuple-element.24), channel_id=1, source_target_pairs={{0,1},{1,0},{2,3},{3,2},{4,5},{5,4},{6,7},{7,6},{8,9},{9,8},{10,11... | collective-permute-start | bytes 6152 | tf_op jit(solution)/shard_map/ppermute | solution.py:136
  30.5 5.3 %collective-permute-start.11 = (bf16[272,768]{1,0:T(8,128)(2,1)S(1)}, bf16[272,768]{1,0:T(8,128)(2,1)S(1)}, u32[]{:S(2)}, u32[]{:S(2)}) collective-permute-start(bf16[272,768]{1,0:T(8,128)(2,1)S(1)} %collective-permute-done.9.refs_5_), channel_id=1, source_target_pairs={{0,1},{1,0},{2,3},{3,2},{4,5},{5,4},{6,7},{7,6},{8,9},{9,8},{10,11... | collective-permute-start | bytes 1253384 | tf_op jit(solution)/shard_map/ppermute | solution.py:136
  30.5 8.4 %all-to-all-start = ((f32[4,1,256]{2,1,0:T(1,128)}), f32[4,1,256]{2,1,0:T(1,128)S(1)}, u32[]{:S(2)}, u32[]{:S(2)}) async-start(f32[4,1,256]{2,1,0:T(1,128)} %get-tuple-element.28), calls=%async_computation | async-start | bytes 8192 | tf_op jit(solution)/shard_map/all_to_all | solution.py:202
  34.8 4.5 %collective-permute-start.10 = (f32[1,1,256]{2,1,0:T(1,128)S(1)}, f32[1,1,256]{2,1,0:T(1,128)S(1)}, u32[]{:S(2)}, u32[]{:S(2)}) collective-permute-start(f32[1,1,256]{2,1,0:T(1,128)S(1)} %compare_half_way.1), channel_id=1, source_target_pairs={{0,16},{8,24},{16,0},{24,8},{1,17},{9,25},{17,1},{25,9},{2,18},{10... | collective-permute-start | bytes 3080 | tf_op jit(solution)/shard_map/ppermute | solution.py:142
  34.9 4.5 %collective-permute-start.8 = (f32[1,1,256]{2,1,0:T(1,128)S(1)}, f32[1,1,256]{2,1,0:T(1,128)S(1)}, u32[]{:S(2)}, u32[]{:S(2)}) collective-permute-start(f32[1,1,256]{2,1,0:T(1,128)S(1)} %bitcast.19), channel_id=1, source_target_pairs={{0,24},{8,0},{16,8},{24,16},{1,25},{9,1},{17,9},{25,17},{2,26},{10... | collective-permute-start | bytes 3080 | tf_op jit(solution)/shard_map/ppermute | solution.py:142
  36.3 4.0 %collective-permute-start.12 = (f32[1,1,256]{2,1,0:T(1,128)S(1)}, f32[1,1,256]{2,1,0:T(1,128)S(1)}, u32[]{:S(2)}, u32[]{:S(2)}) collective-permute-start(f32[1,1,256]{2,1,0:T(1,128)S(1)} %compare_twin.1), channel_id=1, source_target_pairs={{0,17},{1,16},{2,19},{3,18},{4,21},{5,20},{6,23},{7,22},{8,25},{9,... | collective-permute-start | bytes 3080 | tf_op jit(solution)/shard_map/ppermute | solution.py:146
